TPU v7x, 256 devices: a whole 4x4x8 slice. The times are simulated.
256 devices in a mesh: frame: 32 (over z, y), tok: 8 (over x, core).
Axes of the slice: x: 4, y: 4, z: 8, core: 2. Of those that a mesh axis runs over, the one named last changes fastest.
Arguments:
- queries: bfloat16 [32, 1024, 256], P('frame', 'tok'), may hold values from -120 to 120
- keys: bfloat16 [32, 1024, 256], P('frame', 'tok'), may hold values from -4 to 4
- values: bfloat16 [32, 1024, 256], P('frame', 'tok'), may hold values from -6 to 6
- band: int32 [32, 32], replicated, may hold values from -1 to 7, as said below
Outputs:
- attended: bfloat16 [32, 1024, 256], P('frame', 'tok')
Inputs may be any that keep to these rules, and one draw needn't show every extreme that they name: band[i, i] = 7; for |i - j| = 1 the value is 4 or more; for |i - j| >= 2 it is -1 or 0.
All inputs are finite; a program needn't handle non-finite values.
Results may differ from a plain program's by a relative error of at most 0.012.
Values may be sent and summed in bfloat16 or wider, within the bound.
A program may use at most 64 MiB of HBM per device.

v0:
```python
import jax
import jax.numpy as jnp
from jax import lax
from jax.sharding import PartitionSpec as P

HEADS = 2


NEG = -1e30


def padded(shard, sides, width):
    for axis, dim in sides:
        size, length = (lax.axis_size(axis), shard.shape[dim])
        up = [(i, (i + 1) % size) for i in range(size - 1)]
        down = [(j, i) for i, j in up]
        last = lax.slice_in_dim(shard, length - width, length, axis=dim)
        leading = lax.slice_in_dim(shard, 0, width, axis=dim)
        before = lax.ppermute(last, axis, up)
        after = lax.ppermute(leading, axis, down)
        shard = jnp.concatenate([before, shard, after], axis=dim)
    return shard


def scores_part(q_heads, k_rows, v_rows, mask, scale):
    scores = jnp.einsum("qhd,khd->hqk", q_heads, k_rows, preferred_element_type=jnp.float32) * scale
    scores = jnp.where(mask[None, None, :], scores, NEG)
    top = jnp.max(scores, axis=2)
    weights = jnp.exp(scores - top[:, :, None]) * mask[None, None, :].astype(jnp.float32)
    total = jnp.sum(weights, axis=2)
    acc = jnp.einsum(
        "hqk,khd->qhd", weights.astype(jnp.bfloat16), v_rows, preferred_element_type=jnp.float32
    )
    return (top, total, acc)


def rescale(acc, factor):
    return acc * jnp.transpose(factor)[:, :, None]


def combine(first, second):
    top = jnp.maximum(first[0], second[0])
    first_factor = jnp.exp(first[0] - top)
    second_factor = jnp.exp(second[0] - top)
    total = first[1] * first_factor + second[1] * second_factor
    acc = rescale(first[2], first_factor) + rescale(second[2], second_factor)
    return (top, total, acc)


def shards(queries, keys, values, band):
    rows = queries.shape[1]
    width = queries.shape[2]
    heads = HEADS
    depth = width // heads
    scale = depth ** (-0.5)
    frame_count = lax.axis_size("frame")
    frame_id = lax.axis_index("frame")
    block_id = lax.axis_index("tok")
    q_heads = queries[0].reshape(rows, heads, depth)
    packed = jnp.stack((keys, values), axis=2)
    band_row = lax.dynamic_index_in_dim(band, frame_id, 0, keepdims=False)
    whole = lax.all_gather(packed, "tok", axis=1, tiled=True)
    near = padded(whole, (("frame", 0),), 1)
    span = near.shape[1]
    block_of = jnp.arange(span, dtype=jnp.int32) // rows
    empty = (
        jnp.full((heads, rows), NEG, jnp.float32),
        jnp.zeros((heads, rows), jnp.float32),
        jnp.zeros((rows, heads, depth), jnp.float32),
    )
    state = empty
    for offset in range(3):
        other = frame_id - 1 + offset
        inside = (other >= 0) & (other < frame_count)
        reach = band_row[jnp.clip(other, 0, frame_count - 1)]
        mask = inside & (jnp.abs(block_id - block_of) <= reach)
        if offset != 1:
            mask = mask & (block_of != block_id)
        k_rows = near[offset, :, 0].reshape(span, heads, depth)
        v_rows = near[offset, :, 1].reshape(span, heads, depth)
        state = combine(state, scores_part(q_heads, k_rows, v_rows, mask, scale))
    piece = lax.all_gather(packed, "frame", axis=0, tiled=True)
    count = piece.shape[0]
    index = jnp.arange(count, dtype=jnp.int32)
    keep = (index != frame_id) & (band_row >= 0)
    mask = jnp.repeat(keep, piece.shape[1])
    k_rows = piece[:, :, 0].reshape(count * piece.shape[1], heads, depth)
    v_rows = piece[:, :, 1].reshape(count * piece.shape[1], heads, depth)
    far_state = combine(empty, scores_part(q_heads, k_rows, v_rows, mask, scale))
    final = combine(state, far_state)
    result = final[2] / jnp.transpose(final[1])[:, :, None]
    return result.reshape(1, rows, width).astype(jnp.bfloat16)


def solution(mesh):
    in_specs = (P("frame", "tok", None), P("frame", "tok", None), P("frame", "tok", None), P())
    out_specs = P("frame", "tok", None)
    return jax.shard_map(shards, mesh=mesh, in_specs=in_specs, out_specs=out_specs, check_vma=False)
```

profile of v0, /device:TPU:6, one launch (start us, length us, event | category | flops | bytes accessed | tf_op | source)
XLA Modules:
  0.0 150.9 jit_solution(14155052181507887108)
XLA Ops:
  6.5 0.9 copy.36
  7.5 1.0 copy.35
  8.5 0.7 pad_maximum_fusion
  9.2 1.7 %copy.46 = bf16[1,128,2,256]{3,1,2,0:T(8,128)(2,1)} copy(bf16[1,128,2,256]{1,3,2,0:T(8,128)(2,1)} %pad_maximum_fusion) | data formatting | bytes 262144 | tf_op jit(solution)/shard_map/stack | solution.py:60
  10.9 0.9 reshape_squeeze.28
  11.8 1.5 fusion.110
  13.2 0.6 fusion.100
  13.9 23.6 %all-gather.3.cloned.1.call-done = bf16[1,1024,2,256]{1,3,2,0:T(8,128)(2,1)} async-done(((bf16[1,128,2,256]{1,3,2,0:T(8,128)(2,1)}), bf16[1,1024,2,256]{1,3,2,0:T(8,128)(2,1)}) %all-gather.3.cloned.1.call-update) | async-done | bytes 1048592 | tf_op jit(solution)/shard_map/all_gather | solution.py:62
  37.5 1.3 collective-permute-start.1
  38.7 0.7 bitcast_and_fusion
  39.4 0.7 fusion.102
  40.1 0.6 fusion.104
  40.8 4.6 %collective-permute-start = (bf16[1,1024,2,256]{1,3,2,0:T(8,128)(2,1)}, bf16[1,1024,2,256]{1,3,2,0:T(8,128)(2,1)S(1)}, u32[]{:S(2)}, u32[]{:S(2)}) collective-permute-start(bf16[1,1024,2,256]{1,3,2,0:T(8,128)(2,1)} %all-gather.3.cloned.1.call-done), channel_id=1, source_target_pairs={{0,8},{8,16},{16,24},{24,32},{32,40},{40,48},{48,56},{56,64},{64,7... | collective-permute-start | bytes 3145736 | tf_op jit(solution)/shard_map/ppermute | solution.py:19
  45.4 2.1 %fusion.109 = (bf16[1,1024,1,256]{1,3,2,0:T(8,128)(2,1)}, bf16[1,1024,1,256]{1,3,2,0:T(8,128)(2,1)S(1)}) fusion(bf16[1,1024,2,256]{1,3,2,0:T(8,128)(2,1)} %all-gather.3.cloned.1.call-done), kind=kLoop, calls=%fused_computation.119 | loop fusion | bytes 2097152 | tf_op jit(solution)/shard_map/slice | solution.py:80
  47.5 0.4 fusion.114
  47.9 18.4 %collective-permute-done.1 = bf16[1,1024,2,256]{1,3,2,0:T(8,128)(2,1)S(1)} collective-permute-done((bf16[1,1024,2,256]{1,3,2,0:T(8,128)(2,1)}, bf16[1,1024,2,256]{1,3,2,0:T(8,128)(2,1)S(1)}, u32[]{:S(2)}, u32[]{:S(2)}) %collective-permute-start.1) | collective-permute-done | bytes 1048608 | tf_op jit(solution)/shard_map/ppermute | solution.py:20
  66.3 0.9 fusion.107
  67.3 0.4 fusion.112
  67.9 2.2 %collective-permute-done = bf16[1,1024,2,256]{1,3,2,0:T(8,128)(2,1)S(1)} collective-permute-done((bf16[1,1024,2,256]{1,3,2,0:T(8,128)(2,1)}, bf16[1,1024,2,256]{1,3,2,0:T(8,128)(2,1)S(1)}, u32[]{:S(2)}, u32[]{:S(2)}) %collective-permute-start) | collective-permute-done | bytes 1048608 | tf_op jit(solution)/shard_map/ppermute | solution.py:19
  70.2 0.9 fusion.108
  71.0 0.4 fusion.113
  71.8 51.7 %all-gather.5.cloned.1.call-done = bf16[32,128,2,256]{3,1,2,0:T(8,128)(2,1)} async-done(((bf16[1,128,2,256]{3,1,2,0:T(8,128)(2,1)}), bf16[32,128,2,256]{3,1,2,0:T(8,128)(2,1)}) %all-gather.5.cloned.1.call-update) | async-done | bytes 4194320 | tf_op jit(solution)/shard_map/all_gather | solution.py:82
  123.6 4.7 %fusion.106 = (bf16[32,128,1,256]{3,1,2,0:T(8,128)(2,1)}, bf16[32,128,1,256]{3,1,2,0:T(8,128)(2,1)}) fusion(bf16[32,128,2,256]{3,1,2,0:T(8,128)(2,1)} %all-gather.5.cloned.1.call-done), kind=kLoop, calls=%fused_computation.116 | loop fusion | bytes 8388608 | tf_op jit(solution)/shard_map/slice | solution.py:88
  128.3 4.0 %reshape.85 = bf16[4096,2,128]{2,1,0:T(2,128)(2,1)} reshape(bf16[32,128,1,256]{3,1,2,0:T(8,128)(2,1)} %get-tuple-element.19) | data formatting | bytes 4194304 | tf_op jit(solution)/shard_map/reshape;squeeze | solution.py:87
  132.2 4.0 %reshape.86 = bf16[4096,2,128]{2,1,0:T(2,128)(2,1)} reshape(bf16[32,128,1,256]{3,1,2,0:T(8,128)(2,1)} %get-tuple-element.18) | data formatting | bytes 4194304 | tf_op jit(solution)/shard_map/reshape;squeeze | solution.py:88
  136.2 3.3 %fusion.111 = (f32[2,128]{1,0:T(2,128)S(1)}, f32[2,128,4096]{1,2,0:T(8,128)S(1)}) fusion(bf16[128,2,128]{2,1,0:T(2,128)(2,1)S(1)} %reshape_squeeze.28, bf16[4096,2,128]{2,1,0:T(2,128)(2,1)} %reshape.85, pred[4096]{0:T(1024)(128)(4,1)S(1)} %get-tuple-element.42), kind=kOutput, calls=%fused_computation.121 | convolution fusion | flops 271580928 | bytes 6362112 | tf_op jit(solution)/shard_map/qhd,khd->hqk/dot_general | solution.py:26
  139.4 0.8 fusion.2
  140.3 0.5 fusion.18
  141.0 1.4 fusion.42
  142.4 0.5 fusion.26
  142.9 0.5 fusion.47
  143.4 0.7 copy.52
  (17 shorter events, 1.1 us)
Async XLA Ops:
  6.5 30.9 %all-gather.3.cloned.1.call-start = ((), (), s32[]{:S(2)}) async-start(), calls=%async_computation | async-start | bytes 1179648 | tf_op jit(solution)/shard_map/all_gather | solution.py:62
  9.1 114.4 %all-gather.5.cloned.1.call-start = ((), (), s32[]{:S(2)}) async-start(), calls=%async_computation.1 | async-start | bytes 4325376 | tf_op jit(solution)/shard_map/all_gather | solution.py:82
  37.5 28.9 %collective-permute-start.1 = (bf16[1,1024,2,256]{1,3,2,0:T(8,128)(2,1)}, bf16[1,1024,2,256]{1,3,2,0:T(8,128)(2,1)S(1)}, u32[]{:S(2)}, u32[]{:S(2)}) collective-permute-start(bf16[1,1024,2,256]{1,3,2,0:T(8,128)(2,1)} %all-gather.3.cloned.1.call-done), channel_id=1, source_target_pairs={{8,0},{16,8},{24,16},{32,24},{40,32},{48,40},{56,48},{64,56},{72,6... | collective-permute-start | bytes 3145736 | tf_op jit(solution)/shard_map/ppermute | solution.py:20
  40.8 29.4 %collective-permute-start = (bf16[1,1024,2,256]{1,3,2,0:T(8,128)(2,1)}, bf16[1,1024,2,256]{1,3,2,0:T(8,128)(2,1)S(1)}, u32[]{:S(2)}, u32[]{:S(2)}) collective-permute-start(bf16[1,1024,2,256]{1,3,2,0:T(8,128)(2,1)} %all-gather.3.cloned.1.call-done), channel_id=1, source_target_pairs={{0,8},{8,16},{16,24},{24,32},{32,40},{40,48},{48,56},{56,64},{64,7... | collective-permute-start | bytes 3145736 | tf_op jit(solution)/shard_map/ppermute | solution.py:19
  136.2 4.1 %copy-start.2 = (bf16[1,1024,1,256]{1,3,2,0:T(8,128)(2,1)S(1)}, bf16[1,1024,1,256]{1,3,2,0:T(8,128)(2,1)}, u32[]{:S(2)}) copy-start(bf16[1,1024,1,256]{1,3,2,0:T(8,128)(2,1)} %get-tuple-element.24) | copy-start | bytes 1572868
  139.4 1.6 %copy-start = (bf16[4096,2,128]{2,1,0:T(2,128)(2,1)S(1)}, bf16[4096,2,128]{2,1,0:T(2,128)(2,1)}, u32[]{:S(2)}) copy-start(bf16[4096,2,128]{2,1,0:T(2,128)(2,1)} %reshape.86) | copy-start | bytes 6291460
  140.2 2.2 %copy-start.1 = (bf16[1,1024,1,256]{1,3,2,0:T(8,128)(2,1)S(1)}, bf16[1,1024,1,256]{1,3,2,0:T(8,128)(2,1)}, u32[]{:S(2)}) copy-start(bf16[1,1024,1,256]{1,3,2,0:T(8,128)(2,1)} %get-tuple-element.22) | copy-start | bytes 1572868
  141.0 1.9 %copy-start.3 = (bf16[1,1024,1,256]{1,3,2,0:T(8,128)(2,1)S(1)}, bf16[1,1024,1,256]{1,3,2,0:T(8,128)(2,1)}, u32[]{:S(2)}) copy-start(bf16[1,1024,1,256]{1,3,2,0:T(8,128)(2,1)} %get-tuple-element.20) | copy-start | bytes 1572868
Sparse Core Ops, SparseCore 0:
  9.3 28.1 all-gather.2
  40.0 83.4 all-gather.4
where the time goes:
time: 152 us; the launch traced here: 151 us
  waiting for transfers between devices  96 us (63%)
  local copies, waits for them, and re-layouts  23.4 us (15%)
  between operations  13.6 us (9%)
  matrix products  7.31 us (5%)
  starting transfers between devices  5.93 us (4%)
  other arithmetic  4.73 us (3%)
    all_gather x1, waiting for transfers between devices, shards(): piece = lax.all_gather(packed, 'frame', axis=0, tiled=True)  51.7 us
    all_gather x1, waiting for transfers between devices, shards(): whole = lax.all_gather(packed, 'tok', axis=1, tiled=True)  23.6 us
    ppermute x1, waiting for transfers between devices, padded(): after = lax.ppermute(leading, axis, down)  18.4 us
    slice x1, local copies, waits for them, and re-layouts, shards(): v_rows = piece[:, :, 1].reshape(count * piece.shape[1], heads, depth)  4.69 us
    ppermute x1, starting transfers between devices, padded(): before = lax.ppermute(last, axis, up)  4.6 us
    dot_general x4, matrix products, scores_part(): jnp.einsum('qhd,khd->hqk', q_heads, k_rows, preferred_element_type=jnp.fl...  4.53 us
    another operation x1, local copies, waits for them, and re-layouts, shards(): v_rows = piece[:, :, 1].reshape(count * piece.shape[1], heads, depth)  3.95 us
    another operation x1, local copies, waits for them, and re-layouts, shards(): k_rows = piece[:, :, 0].reshape(count * piece.shape[1], heads, depth)  3.95 us
  transfers between devices with their start and end apart: 4, of which 4 were waited for; matrix products, arithmetic and copies ran while one was open for 8% of the time, Pallas kernels for 0%

commit v1 on v0

v1 whole, which is shorter than its diff:
```python
import functools
import math

import jax
import jax.numpy as jnp
from jax import lax
from jax.experimental import pallas as pl
from jax.experimental.pallas import tpu as pltpu
from jax.sharding import PartitionSpec as P

HEADS = 2
HD = 128
ROWS = 128
ZN, YN, XN, CN = 8, 4, 4, 2
FRAMES = ZN * YN
FAR, NEAR = 0, 1
HIDE = -1e30
LOW = -1e29
EXP2_SCALE = HD ** -0.5 * math.log2(math.e)


def coords():
    frame = lax.axis_index("frame")
    tok = lax.axis_index("tok")
    return lax.div(frame, YN), lax.rem(frame, YN), lax.div(tok, CN), lax.rem(tok, CN)


def kernel(
    q_ref, k_ref, v_ref, band_ref, o_ref,
    kvz, kvn, q_own, q_set, bias, acc, top, total,
    o_send, st_send, o_recv, st_recv,
    z_ss, z_rs, n_ss, n_rs, q_ss, q_rs, o_ss, o_rs, s_ss, s_rs,
):
    z, y, x, c = coords()

    def at(dz=0, dy=0, dx=0, dc=0):
        frame = lax.rem(z + (dz + ZN), ZN) * YN + lax.rem(y + (dy + YN), YN)
        tok = lax.rem(x + (dx + XN), XN) * CN + lax.rem(c + dc, CN)
        return (frame, tok)

    def remote(src, dst, ss, rs, to):
        return pltpu.make_async_remote_copy(
            src_ref=src, dst_ref=dst, send_sem=ss, recv_sem=rs,
            device_id=to, device_id_type=pl.DeviceIdType.MESH,
        )

    started = []

    def go(copy):
        copy.start()
        started.append(copy)

    def z_copy(slot, h, src_slot, dz):
        return remote(kvz.at[src_slot, h], kvz.at[slot, h], z_ss.at[slot, h], z_rs.at[slot, h], at(dz=dz))

    def n_copy(slot, src, **to):
        return remote(src, kvn.at[slot], n_ss.at[slot], n_rs.at[slot], at(**to))

    def q_copy(part, k, n):
        to = at(dy=k) if part == FAR else at(dx=k)
        return remote(q_own, q_set.at[part, n - k - 1], q_ss.at[part, n - k - 1], q_rs.at[part, n - k - 1], to)

    def o_copies(part, k, n, h):
        to = at(dy=k) if part == FAR else at(dx=k)
        there = n - k - 1
        return (
            remote(o_send.at[part, k - 1, h], o_recv.at[part, there, h], o_ss.at[part, there, h], o_rs.at[part, there, h], to),
            remote(st_send.at[part, k - 1, h], st_recv.at[part, there, h], s_ss.at[part, there, h], s_rs.at[part, there, h], to),
        )

    barrier = pltpu.get_barrier_semaphore()
    peers = [at(dz=1), at(dz=-1), at(dz=2), at(dz=-2), at(dy=1), at(dy=2), at(dy=3), at(dx=1), at(dx=2), at(dx=3), at(dc=1)]
    for peer in peers:
        pl.semaphore_signal(barrier, inc=1, device_id=peer, device_id_type=pl.DeviceIdType.MESH)

    for h in range(HEADS):
        cols = slice(h * HD, (h + 1) * HD)
        kvz[0, h, 0:ROWS] = k_ref[:, cols]
        kvz[0, h, ROWS:2 * ROWS] = v_ref[:, cols].T
        q_own[h] = q_ref[:, cols].T

    lane = lax.broadcasted_iota(jnp.int32, (1, 4 * ROWS), 1) // ROWS

    def row_of(cells):
        row = jnp.full((1, 4 * ROWS), cells[0], jnp.float32)
        for k in range(1, 4):
            row = jnp.where(lane == k, cells[k], row)
        return row

    frame = z * YN + y
    for slot in range(ZN):
        key_frame = lax.rem(z + (ZN - slot), ZN) * YN + y
        cells = []
        for k in range(YN):
            query_frame = z * YN + lax.rem(y + k, YN)
            seen = (jnp.abs(query_frame - key_frame) >= 2) & (band_ref[query_frame, key_frame] >= 0)
            cells.append(jnp.where(seen, 0.0, HIDE).astype(jnp.float32))
        bias[slot] = row_of(cells)
    for step in range(3):
        key_frame = frame + (step - 1)
        inside = (key_frame >= 0) & (key_frame < FRAMES)
        reach = band_ref[frame, jnp.clip(key_frame, 0, FRAMES - 1)]
        for other in range(CN):
            key_block = x * CN + lax.rem(c + other, CN)
            cells = []
            for k in range(XN):
                query_block = lax.rem(x + k, XN) * CN + c
                seen = inside & (jnp.abs(query_block - key_block) <= reach)
                cells.append(jnp.where(seen, 0.0, HIDE).astype(jnp.float32))
            bias[ZN + step * CN + other] = row_of(cells)

    pl.semaphore_wait(barrier, len(peers))

    for h in range(HEADS):
        go(z_copy(1, h, 0, 1))
        go(z_copy(7, h, 0, -1))
    for k in (2, 1, 3):
        go(q_copy(FAR, k, YN))
        go(q_copy(NEAR, k, XN))
    go(n_copy(0, kvz.at[0], dc=1))
    before = n_copy(1, kvz.at[0], dy=1)
    after = n_copy(3, kvz.at[0], dy=-1)
    started.extend([before, after])

    @pl.when(y < YN - 1)
    def _():
        before.start()

    @pl.when(y > 0)
    def _():
        after.start()

    def update(part, h, blocks, first):
        heads = [q_own[h]] + [q_set[part, k, h] for k in range(3)]
        qt = jnp.concatenate(heads, axis=1)
        rows = [bias[b] for _, b in blocks]
        scores = [jnp.dot(ref[0:ROWS], qt, preferred_element_type=jnp.float32) for ref, _ in blocks]
        high = functools.reduce(jnp.maximum, [jnp.max(s, axis=0, keepdims=True) + r for s, r in zip(scores, rows)])
        old = jnp.full((1, 4 * ROWS), LOW, jnp.float32) if first else top[part, h]
        new = jnp.maximum(old, high)
        weights = [jnp.exp2((s - (new - r)) * EXP2_SCALE) for s, r in zip(scores, rows)]
        add = functools.reduce(jnp.add, [jnp.sum(w, axis=0, keepdims=True) for w in weights])
        wt = jnp.concatenate([w.astype(jnp.bfloat16) for w in weights], axis=0)
        vt = jnp.concatenate([ref[ROWS:2 * ROWS] for ref, _ in blocks], axis=1)
        out = jnp.dot(vt, wt, preferred_element_type=jnp.float32)
        top[part, h] = new
        if first:
            total[part, h] = add
            acc[part, h] = out
        else:
            factor = jnp.exp2((old - new) * EXP2_SCALE)
            total[part, h] = total[part, h] * factor + add
            acc[part, h] = acc[part, h] * factor + out

    def far(h, slots, first=False):
        update(FAR, h, [(kvz.at[s, h], s) for s in slots], first)

    def near(h, refs, first=False):
        update(NEAR, h, [(ref.at[h], b) for ref, b in refs], first)

    def send_out(part, h, n):
        for k in (2, 1, 3):
            cols = slice(k * ROWS, (k + 1) * ROWS)
            o_send[part, k - 1, h] = acc[part, h, :, cols].astype(jnp.bfloat16)
            st_send[part, k - 1, h] = jnp.concatenate(
                [top[part, h, :, cols], total[part, h, :, cols], jnp.zeros((6, ROWS), jnp.float32)], axis=0
            )
            for copy in o_copies(part, k, n, h):
                go(copy)

    def z_wait(slot, h):
        z_copy(slot, h, 0, 1).wait_recv()

    for h in range(HEADS):
        z_wait(1, h)
        go(z_copy(2, h, 1, 1))
        z_wait(7, h)
        go(z_copy(6, h, 7, -1))

    @pl.when(y == YN - 1)
    def _():
        n_copy(1, kvz.at[1], dy=1).start()

    @pl.when(y == 0)
    def _():
        n_copy(3, kvz.at[7], dy=-1).start()

    n_copy(0, kvz.at[0], dc=1).wait_recv()
    for k in range(1, XN):
        q_copy(NEAR, k, XN).wait_recv()
    for h in range(HEADS):
        near(h, [(kvz.at[0], ZN + 2), (kvn.at[0], ZN + 3)], first=True)
    for k in range(1, YN):
        q_copy(FAR, k, YN).wait_recv()
    for h in range(HEADS):
        far(h, (0, 1, 7), first=True)

    for slot in (1, 3):
        n_copy(slot, kvz.at[0], dy=1).wait_recv()
        go(n_copy(slot + 1, kvn.at[slot], dc=1))

    for h in range(HEADS):
        z_wait(2, h)
        if h == 0:
            go(z_copy(4, h, 2, 2))
        go(z_copy(3, h, 2, 1))
        z_wait(6, h)
        if h == 1:
            go(z_copy(4, h, 6, -2))
        go(z_copy(5, h, 6, -1))

    for slot in (2, 4):
        n_copy(slot, kvz.at[0], dc=1).wait_recv()
    for h in range(HEADS):
        near(h, [(kvn.at[1], ZN), (kvn.at[2], ZN + 1)])
        near(h, [(kvn.at[3], ZN + 4), (kvn.at[4], ZN + 5)])
        send_out(NEAR, h, XN)
    for h in range(HEADS):
        far(h, (2, 6))
    for h in range(HEADS):
        z_wait(3, h)
        z_wait(5, h)
        far(h, (3, 5))
    for h in range(HEADS):
        z_wait(4, h)
        far(h, (4,))
        send_out(FAR, h, YN)

    def merged(h, state, parts):
        for part in parts:
            for k in range(3):
                for copy in o_copies(part, k + 1, 4, h):
                    copy.wait_recv()
        high, count, out = state
        tops = [high] + [st_recv[part, k, h, 0:1] for part in parts for k in range(3)]
        counts = [count] + [st_recv[part, k, h, 1:2] for part in parts for k in range(3)]
        outs = [out] + [o_recv[part, k, h].astype(jnp.float32) for part in parts for k in range(3)]
        new = functools.reduce(jnp.maximum, tops)
        factors = [jnp.exp2((t - new) * EXP2_SCALE) for t in tops]
        count = functools.reduce(jnp.add, [n * f for n, f in zip(counts, factors)])
        out = functools.reduce(jnp.add, [o * f for o, f in zip(outs, factors)])
        return new, count, out

    own = slice(0, ROWS)
    states = []
    for h in range(HEADS):
        one = (top[NEAR, h, :, own], total[NEAR, h, :, own], acc[NEAR, h, :, own])
        two = (top[FAR, h, :, own], total[FAR, h, :, own], acc[FAR, h, :, own])
        new = jnp.maximum(one[0], two[0])
        f1 = jnp.exp2((one[0] - new) * EXP2_SCALE)
        f2 = jnp.exp2((two[0] - new) * EXP2_SCALE)
        states.append(merged(h, (new, one[1] * f1 + two[1] * f2, one[2] * f1 + two[2] * f2), (NEAR,)))
    for h in range(HEADS):
        _, count, out = merged(h, states[h], (FAR,))
        o_ref[:, h * HD:(h + 1) * HD] = (out / count).T.astype(jnp.bfloat16)
    for copy in started:
        copy.wait_send()


def shards(queries, keys, values, band):
    vmem = pl.BlockSpec(memory_space=pltpu.VMEM)
    bf16, f32 = jnp.bfloat16, jnp.float32
    dma = pltpu.SemaphoreType.DMA
    out = pl.pallas_call(
        kernel,
        out_shape=jax.ShapeDtypeStruct((ROWS, HEADS * HD), bf16),
        in_specs=[vmem, vmem, vmem, pl.BlockSpec(memory_space=pltpu.SMEM)],
        out_specs=vmem,
        scratch_shapes=[
            pltpu.VMEM((ZN, HEADS, 2 * ROWS, HD), bf16),
            pltpu.VMEM((5, HEADS, 2 * ROWS, HD), bf16),
            pltpu.VMEM((HEADS, HD, ROWS), bf16),
            pltpu.VMEM((2, 3, HEADS, HD, ROWS), bf16),
            pltpu.VMEM((ZN + 6, 1, 4 * ROWS), f32),
            pltpu.VMEM((2, HEADS, HD, 4 * ROWS), f32),
            pltpu.VMEM((2, HEADS, 1, 4 * ROWS), f32),
            pltpu.VMEM((2, HEADS, 1, 4 * ROWS), f32),
            pltpu.VMEM((2, 3, HEADS, HD, ROWS), bf16),
            pltpu.VMEM((2, 3, HEADS, 8, ROWS), f32),
            pltpu.VMEM((2, 3, HEADS, HD, ROWS), bf16),
            pltpu.VMEM((2, 3, HEADS, 8, ROWS), f32),
            dma((ZN, HEADS)), dma((ZN, HEADS)),
            dma((5,)), dma((5,)),
            dma((2, 3)), dma((2, 3)),
            dma((2, 3, HEADS)), dma((2, 3, HEADS)),
            dma((2, 3, HEADS)), dma((2, 3, HEADS)),
        ],
        compiler_params=pltpu.CompilerParams(collective_id=0, has_side_effects=True, vmem_limit_bytes=32 * 2 ** 20),
    )(queries[0], keys[0], values[0], band)
    return out[None]


def solution(mesh):
    spec = P("frame", "tok", None)
    return jax.shard_map(shards, mesh=mesh, in_specs=(spec, spec, spec, P()), out_specs=spec, check_vma=False)
```

time: 152 us -> 34.5 us (0.23)
  waiting for transfers between devices: 96 us -> 0 us
  Pallas kernels: 0 us -> 30 us
  local copies, waits for them, and re-layouts: 23.4 us -> 3.87 us
  between operations: 13.6 us -> 0.01 us
  matrix products: 7.31 us -> 0 us
  starting transfers between devices: 5.93 us -> 0 us
  other arithmetic: 4.73 us -> 0 us
    all_gather x2 -> x0, waiting for transfers between devices: 75.3 us -> none  [the longest x1 51.7 us: shards(): piece = lax.all_gather(packed, 'frame', axis=0, tiled=True)]
    pallas_call x0 -> x1, Pallas kernels: none -> 30 us  [shards(): pl.pallas_call(kernel, out_shape=jax.ShapeDtypeStruct((ROWS, HEADS * HD),...]
    ppermute x2 -> x0, waiting for transfers between devices: 20.7 us -> none  [the longest x1 18.4 us: padded(): after = lax.ppermute(leading, axis, down)]
    another operation x4 -> x0, local copies, waits for them, and re-layouts: 10.4 us -> none  [the longest x1 3.95 us: shards(): v_rows = piece[:, :, 1].reshape(count * piece.shape[1], heads, depth)]
    slice x4 -> x0, local copies, waits for them, and re-layouts: 8.56 us -> none  [the longest x1 4.69 us: shards(): v_rows = piece[:, :, 1].reshape(count * piece.shape[1], heads, depth)]
    dot_general x8 -> x0, matrix products: 7.31 us -> none  [the longest x4 4.53 us: scores_part(): jnp.einsum('qhd,khd->hqk', q_heads, k_rows, preferred_element_type=jnp.fl...]
    ppermute x2 -> x0, starting transfers between devices: 5.88 us -> none  [the longest x1 4.6 us: padded(): before = lax.ppermute(last, axis, up)]
    convert_element_type x4 -> x0, other arithmetic: 1.93 us -> none  [scores_part(): mask[None, None, :].astype(jnp.float32)]
  transfers between devices with their start and end apart: 4 -> 0, of which waited for: 4 -> 0; matrix products, arithmetic and copies ran while one was open for 8% -> 0% of each run, Pallas kernels for 0% -> 0%
where the time goes in v1:
time: 34.5 us; the launch traced here: 33.9 us
  Pallas kernels  30 us (87%)
  local copies, waits for them, and re-layouts  3.87 us (11%)
    pallas_call x1, Pallas kernels, shards(): pl.pallas_call(kernel, out_shape=jax.ShapeDtypeStruct((ROWS, HEADS * HD),...  30 us
    unnamed x9, local copies, waits for them, and re-layouts  3.87 us

profile of v1, /device:TPU:6, one launch (start us, length us, event | category | flops | bytes accessed | tf_op | source)
XLA Modules:
  0.0 33.9 jit_solution(1163213233564062443)
XLA Ops:
  0.0 0.0 copy-start
  0.0 0.8 %copy-done = bf16[1,128,256]{2,1,0:T(8,128)(2,1)S(1)} copy-done((bf16[1,128,256]{2,1,0:T(8,128)(2,1)S(1)}, bf16[1,128,256]{2,1,0:T(8,128)(2,1)}, u32[]{:S(2)}) %copy-start) | copy-done | bytes 65560
  0.8 0.0 copy-start.1
  0.8 0.8 %copy-done.1 = bf16[1,128,256]{2,1,0:T(8,128)(2,1)S(1)} copy-done((bf16[1,128,256]{2,1,0:T(8,128)(2,1)S(1)}, bf16[1,128,256]{2,1,0:T(8,128)(2,1)}, u32[]{:S(2)}) %copy-start.1) | copy-done | bytes 65560
  1.7 0.0 copy-start.2
  1.7 0.8 %copy-done.2 = bf16[1,128,256]{2,1,0:T(8,128)(2,1)S(1)} copy-done((bf16[1,128,256]{2,1,0:T(8,128)(2,1)S(1)}, bf16[1,128,256]{2,1,0:T(8,128)(2,1)}, u32[]{:S(2)}) %copy-start.2) | copy-done | bytes 65560
  2.5 0.0 copy-start.3
  2.5 0.7 %copy-done.3 = s32[32,32]{1,0:T(8,128)S(1)} copy-done((s32[32,32]{1,0:T(8,128)S(1)}, s32[32,32]{1,0:T(8,128)}, u32[]{:S(2)}) %copy-start.3) | copy-done | bytes 4120
  3.2 30.0 %shard_map.46 = bf16[128,256]{1,0:T(8,128)(2,1)S(1)} custom-call(bf16[128,256]{1,0:T(8,128)(2,1)S(1)} %bitcast.5, bf16[128,256]{1,0:T(8,128)(2,1)S(1)} %bitcast.6, bf16[128,256]{1,0:T(8,128)(2,1)S(1)} %bitcast.7, s32[32,32]{1,0:T(8,128)S(1)} %copy-done.3), custom_call_target="tpu_custom_call" | custom-call | tf_op jit(solution)/shard_map/pallas_call | solution.py:264
  33.3 0.6 %copy.6 = bf16[1,128,256]{2,1,0:T(8,128)(2,1)} copy(bf16[1,128,256]{2,1,0:T(8,128)(2,1)S(1)} %bitcast.4) | data formatting | bytes 131072
Async XLA Ops:
  0.0 0.8 %copy-start = (bf16[1,128,256]{2,1,0:T(8,128)(2,1)S(1)}, bf16[1,128,256]{2,1,0:T(8,128)(2,1)}, u32[]{:S(2)}) copy-start(bf16[1,128,256]{2,1,0:T(8,128)(2,1)} %param.4) | copy-start | bytes 196612
  0.8 0.8 %copy-start.1 = (bf16[1,128,256]{2,1,0:T(8,128)(2,1)S(1)}, bf16[1,128,256]{2,1,0:T(8,128)(2,1)}, u32[]{:S(2)}) copy-start(bf16[1,128,256]{2,1,0:T(8,128)(2,1)} %param.5) | copy-start | bytes 196612
  1.7 0.8 %copy-start.2 = (bf16[1,128,256]{2,1,0:T(8,128)(2,1)S(1)}, bf16[1,128,256]{2,1,0:T(8,128)(2,1)}, u32[]{:S(2)}) copy-start(bf16[1,128,256]{2,1,0:T(8,128)(2,1)} %param.6) | copy-start | bytes 196612
  2.5 0.7 %copy-start.3 = (s32[32,32]{1,0:T(8,128)S(1)}, s32[32,32]{1,0:T(8,128)}, u32[]{:S(2)}) copy-start(s32[32,32]{1,0:T(8,128)} %band_ref.1) | copy-start | bytes 12292

commit v2 on v1

v2 whole, which is shorter than its diff:
```python
import functools
import math

import jax
import jax.numpy as jnp
from jax import lax
from jax.experimental import pallas as pl
from jax.experimental.pallas import tpu as pltpu
from jax.sharding import PartitionSpec as P

HEADS = 2
HD = 128
ROWS = 128
ZN, YN, XN, CN = 8, 4, 4, 2
FRAMES = ZN * YN
FAR, NEAR = 0, 1
K, V = 0, 1
HIDE = -1e30
LOW = -1e29
EXP2_SCALE = HD ** -0.5 * math.log2(math.e)


def coords():
    frame = lax.axis_index("frame")
    tok = lax.axis_index("tok")
    return lax.div(frame, YN), lax.rem(frame, YN), lax.div(tok, CN), lax.rem(tok, CN)


def kernel(
    q_ref, k_ref, v_ref, band_ref, o_ref,
    v_in, q_in, band_in, kz, vz, kn, vn, q_own, q_set, bias, acc, top, total,
    o_send, st_send, o_recv, st_recv,
    in_sem, z_ss, z_rs, n_ss, n_rs, q_ss, q_rs, o_ss, o_rs, s_ss, s_rs,
):
    z, y, x, c = coords()

    def at(dz=0, dy=0, dx=0, dc=0):
        frame = lax.rem(z + (dz + ZN), ZN) * YN + lax.rem(y + (dy + YN), YN)
        tok = lax.rem(x + (dx + XN), XN) * CN + lax.rem(c + dc, CN)
        return (frame, tok)

    def remote(src, dst, ss, rs, to):
        return pltpu.make_async_remote_copy(
            src_ref=src, dst_ref=dst, send_sem=ss, recv_sem=rs,
            device_id=to, device_id_type=pl.DeviceIdType.MESH,
        )

    barrier = pltpu.get_barrier_semaphore()
    peers = [at(dz=1), at(dz=-1), at(dz=2), at(dz=-2), at(dy=1), at(dy=2), at(dy=3), at(dx=1), at(dx=2), at(dx=3), at(dc=1)]
    for peer in peers:
        pl.semaphore_signal(barrier, inc=1, device_id=peer, device_id_type=pl.DeviceIdType.MESH)

    loads = [
        pltpu.make_async_copy(src, dst, in_sem.at[i])
        for i, (src, dst) in enumerate(((v_ref, v_in), (k_ref, kz.at[0]), (q_ref, q_in), (band_ref, band_in)))
    ]
    for load in loads:
        load.start()

    started = []

    def go(copy):
        copy.start()
        started.append(copy)

    def piece(keys, values, h, kind):
        part = pl.ds(h * HD, HD)
        return keys.at[:, part] if kind == K else values.at[part]

    def z_copy(slot, h, kind, src, dz):
        return remote(
            piece(kz.at[src], vz.at[src], h, kind), piece(kz.at[slot], vz.at[slot], h, kind),
            z_ss.at[slot, h, kind], z_rs.at[slot, h, kind], at(dz=dz),
        )

    def z_wait(slot, h, kind):
        z_copy(slot, h, kind, 0, 1).wait_recv()

    def n_copy(slot, h, kind, keys, values, **to):
        return remote(
            piece(keys, values, h, kind), piece(kn.at[slot], vn.at[slot], h, kind),
            n_ss.at[slot, h, kind], n_rs.at[slot, h, kind], at(**to),
        )

    def n_wait(slot, h, kind):
        n_copy(slot, h, kind, kz.at[0], vz.at[0], dc=1).wait_recv()

    def q_copy(part, k, n):
        to = at(dy=k) if part == FAR else at(dx=k)
        return remote(q_own, q_set.at[part, n - k - 1], q_ss.at[part, n - k - 1], q_rs.at[part, n - k - 1], to)

    def o_copies(part, k, n, h):
        to = at(dy=k) if part == FAR else at(dx=k)
        there = n - k - 1
        return (
            remote(o_send.at[part, k - 1, h], o_recv.at[part, there, h], o_ss.at[part, there, h], o_rs.at[part, there, h], to),
            remote(st_send.at[part, k - 1, h], st_recv.at[part, there, h], s_ss.at[part, there, h], s_rs.at[part, there, h], to),
        )

    loads[0].wait()
    vz[0] = v_in[...].T
    loads[1].wait()
    pl.semaphore_wait(barrier, len(peers))

    for kind in (K, V):
        for h in range(HEADS):
            go(z_copy(1, h, kind, 0, 1))
            go(z_copy(7, h, kind, 0, -1))

    loads[2].wait()
    q_own[...] = q_in[...].T
    for k in (2, 1, 3):
        go(q_copy(NEAR, k, XN))
        go(q_copy(FAR, k, YN))
    pieces = [(h, kind) for h in range(HEADS) for kind in (K, V)]
    before = [n_copy(1, h, kind, kz.at[0], vz.at[0], dy=1) for h, kind in pieces]
    after = [n_copy(3, h, kind, kz.at[0], vz.at[0], dy=-1) for h, kind in pieces]
    started.extend(before + after)

    @pl.when(y < YN - 1)
    def _():
        for copy in before:
            copy.start()

    @pl.when(y > 0)
    def _():
        for copy in after:
            copy.start()

    for h, kind in pieces:
        go(n_copy(0, h, kind, kz.at[0], vz.at[0], dc=1))

    loads[3].wait()
    lane = lax.broadcasted_iota(jnp.int32, (1, 4 * ROWS), 1) // ROWS

    def row_of(cells):
        row = jnp.full((1, 4 * ROWS), cells[0], jnp.float32)
        for k in range(1, 4):
            row = jnp.where(lane == k, cells[k], row)
        return row

    frame = z * YN + y
    for slot in range(ZN):
        key_frame = lax.rem(z + (ZN - slot), ZN) * YN + y
        cells = []
        for k in range(YN):
            query_frame = z * YN + lax.rem(y + k, YN)
            seen = (jnp.abs(query_frame - key_frame) >= 2) & (band_in[query_frame, key_frame] >= 0)
            cells.append(jnp.where(seen, 0.0, HIDE).astype(jnp.float32))
        bias[slot] = row_of(cells)
    for step in range(3):
        key_frame = frame + (step - 1)
        inside = (key_frame >= 0) & (key_frame < FRAMES)
        reach = band_in[frame, jnp.clip(key_frame, 0, FRAMES - 1)]
        for other in range(CN):
            key_block = x * CN + lax.rem(c + other, CN)
            cells = []
            for k in range(XN):
                query_block = lax.rem(x + k, XN) * CN + c
                seen = inside & (jnp.abs(query_block - key_block) <= reach)
                cells.append(jnp.where(seen, 0.0, HIDE).astype(jnp.float32))
            bias[ZN + step * CN + other] = row_of(cells)

    def update(part, h, blocks, first):
        cols = pl.ds(h * HD, HD)
        qt = jnp.concatenate([q_own[cols]] + [q_set[part, k, cols] for k in range(3)], axis=1)
        rows = [bias[b] for _, _, b in blocks]
        scores = [jnp.dot(keys[:, cols], qt, preferred_element_type=jnp.float32) for keys, _, _ in blocks]
        high = functools.reduce(jnp.maximum, [jnp.max(s, axis=0, keepdims=True) + r for s, r in zip(scores, rows)])
        old = jnp.full((1, 4 * ROWS), LOW, jnp.float32) if first else top[part, h]
        new = jnp.maximum(old, high)
        weights = [jnp.exp2((s - (new - r)) * EXP2_SCALE) for s, r in zip(scores, rows)]
        add = functools.reduce(jnp.add, [jnp.sum(w, axis=0, keepdims=True) for w in weights])
        wt = jnp.concatenate([w.astype(jnp.bfloat16) for w in weights], axis=0)
        vt = jnp.concatenate([values[cols] for _, values, _ in blocks], axis=1)
        out = jnp.dot(vt, wt, preferred_element_type=jnp.float32)
        top[part, h] = new
        if first:
            total[part, h] = add
            acc[part, h] = out
        else:
            factor = jnp.exp2((old - new) * EXP2_SCALE)
            total[part, h] = total[part, h] * factor + add
            acc[part, h] = acc[part, h] * factor + out

    def far(h, slots, first=False):
        update(FAR, h, [(kz.at[s], vz.at[s], s) for s in slots], first)

    def near(h, refs, first=False):
        update(NEAR, h, [(keys, values, b) for keys, values, b in refs], first)

    def send_out(part, h, n):
        for k in (2, 1, 3):
            cols = slice(k * ROWS, (k + 1) * ROWS)
            o_send[part, k - 1, h] = acc[part, h, :, cols].astype(jnp.bfloat16)
            st_send[part, k - 1, h] = jnp.concatenate(
                [top[part, h, :, cols], total[part, h, :, cols], jnp.zeros((6, ROWS), jnp.float32)], axis=0
            )
            for copy in o_copies(part, k, n, h):
                go(copy)

    for kind in (K, V):
        for h in range(HEADS):
            z_wait(1, h, kind)
            go(z_copy(2, h, kind, 1, 1))

            @pl.when(y == YN - 1)
            def _(h=h, kind=kind):
                n_copy(1, h, kind, kz.at[1], vz.at[1], dy=1).start()

            z_wait(7, h, kind)
            go(z_copy(6, h, kind, 7, -1))

            @pl.when(y == 0)
            def _(h=h, kind=kind):
                n_copy(3, h, kind, kz.at[7], vz.at[7], dy=-1).start()

    for h, kind in pieces:
        n_wait(0, h, kind)
    for k in range(1, XN):
        q_copy(NEAR, k, XN).wait_recv()
    for h in range(HEADS):
        near(h, [(kz.at[0], vz.at[0], ZN + 2), (kn.at[0], vn.at[0], ZN + 3)], first=True)
    for k in range(1, YN):
        q_copy(FAR, k, YN).wait_recv()
    far(0, (0, 1, 7), first=True)

    for h in range(HEADS):
        for kind in (K, V):
            z_wait(2, h, kind)
            go(z_copy(3, h, kind, 2, 1))
            if kind == K:
                go(z_copy(4, h, kind, 2, 2))
            z_wait(6, h, kind)
            go(z_copy(5, h, kind, 6, -1))
            if kind == V:
                go(z_copy(4, h, kind, 6, -2))

    for h, kind in pieces:
        for slot in (1, 3):
            n_wait(slot, h, kind)
            go(n_copy(slot + 1, h, kind, kn.at[slot], vn.at[slot], dc=1))
    far(1, (0, 1, 7), first=True)
    for h in range(HEADS):
        far(h, (2, 6))
    for h in range(HEADS):
        for slot in (2, 4):
            for kind in (K, V):
                n_wait(slot, h, kind)
        near(h, [(kn.at[1], vn.at[1], ZN), (kn.at[2], vn.at[2], ZN + 1)])
        near(h, [(kn.at[3], vn.at[3], ZN + 4), (kn.at[4], vn.at[4], ZN + 5)])
        send_out(NEAR, h, XN)
    for h in range(HEADS):
        for slot in (3, 5, 4):
            for kind in (K, V):
                z_wait(slot, h, kind)
        far(h, (4, 3, 5))
        send_out(FAR, h, YN)

    def merged(h, state, part):
        for k in range(3):
            for copy in o_copies(part, k + 1, 4, h):
                copy.wait_recv()
        high, count, out = state
        tops = [high] + [st_recv[part, k, h, 0:1] for k in range(3)]
        counts = [count] + [st_recv[part, k, h, 1:2] for k in range(3)]
        outs = [out] + [o_recv[part, k, h].astype(jnp.float32) for k in range(3)]
        new = functools.reduce(jnp.maximum, tops)
        factors = [jnp.exp2((t - new) * EXP2_SCALE) for t in tops]
        count = functools.reduce(jnp.add, [n * f for n, f in zip(counts, factors)])
        out = functools.reduce(jnp.add, [o * f for o, f in zip(outs, factors)])
        return new, count, out

    own = slice(0, ROWS)
    states = []
    for h in range(HEADS):
        one = (top[NEAR, h, :, own], total[NEAR, h, :, own], acc[NEAR, h, :, own])
        two = (top[FAR, h, :, own], total[FAR, h, :, own], acc[FAR, h, :, own])
        new = jnp.maximum(one[0], two[0])
        f1 = jnp.exp2((one[0] - new) * EXP2_SCALE)
        f2 = jnp.exp2((two[0] - new) * EXP2_SCALE)
        states.append(merged(h, (new, one[1] * f1 + two[1] * f2, one[2] * f1 + two[2] * f2), NEAR))
    for h in range(HEADS):
        _, count, out = merged(h, states[h], FAR)
        o_ref[:, h * HD:(h + 1) * HD] = (out / count).T.astype(jnp.bfloat16)
    for copy in started:
        copy.wait_send()


def shards(queries, keys, values, band):
    vmem = pl.BlockSpec(memory_space=pltpu.VMEM)
    bf16, f32 = jnp.bfloat16, jnp.float32
    dma = pltpu.SemaphoreType.DMA
    width = HEADS * HD
    out = pl.pallas_call(
        kernel,
        out_shape=jax.ShapeDtypeStruct((ROWS, width), bf16),
        in_specs=[pl.BlockSpec(memory_space=pltpu.HBM)] * 4,
        out_specs=vmem,
        scratch_shapes=[
            pltpu.VMEM((ROWS, width), bf16),
            pltpu.VMEM((ROWS, width), bf16),
            pltpu.SMEM((FRAMES, FRAMES), jnp.int32),
            pltpu.VMEM((ZN, ROWS, width), bf16),
            pltpu.VMEM((ZN, width, ROWS), bf16),
            pltpu.VMEM((5, ROWS, width), bf16),
            pltpu.VMEM((5, width, ROWS), bf16),
            pltpu.VMEM((width, ROWS), bf16),
            pltpu.VMEM((2, 3, width, ROWS), bf16),
            pltpu.VMEM((ZN + 6, 1, 4 * ROWS), f32),
            pltpu.VMEM((2, HEADS, HD, 4 * ROWS), f32),
            pltpu.VMEM((2, HEADS, 1, 4 * ROWS), f32),
            pltpu.VMEM((2, HEADS, 1, 4 * ROWS), f32),
            pltpu.VMEM((2, 3, HEADS, HD, ROWS), bf16),
            pltpu.VMEM((2, 3, HEADS, 8, ROWS), f32),
            pltpu.VMEM((2, 3, HEADS, HD, ROWS), bf16),
            pltpu.VMEM((2, 3, HEADS, 8, ROWS), f32),
            dma((4,)),
            dma((ZN, HEADS, 2)), dma((ZN, HEADS, 2)),
            dma((5, HEADS, 2)), dma((5, HEADS, 2)),
            dma((2, 3)), dma((2, 3)),
            dma((2, 3, HEADS)), dma((2, 3, HEADS)),
            dma((2, 3, HEADS)), dma((2, 3, HEADS)),
        ],
        compiler_params=pltpu.CompilerParams(collective_id=0, has_side_effects=True, vmem_limit_bytes=55100 * 2 ** 10),
    )(queries[0], keys[0], values[0], band)
    return out[None]


def solution(mesh):
    spec = P("frame", "tok", None)
    return jax.shard_map(shards, mesh=mesh, in_specs=(spec, spec, spec, P()), out_specs=spec, check_vma=False)
```

time: 34.5 us -> 30.2 us (0.88)
  the two profiles are of different devices: /device:TPU:6 before, /device:TPU:1 now
where the time goes in v2:
time: 30.2 us; the launch traced here: 30 us
  Pallas kernels  28.7 us (95%)
  local copies, waits for them, and re-layouts  1.35 us (4%)
    pallas_call x1, Pallas kernels, shards(): pl.pallas_call(kernel, out_shape=jax.ShapeDtypeStruct((ROWS, width), bf16...  28.7 us
    unnamed x3, local copies, waits for them, and re-layouts  1.35 us

profile of v2, /device:TPU:1, one launch (start us, length us, event | category | flops | bytes accessed | tf_op | source)
XLA Modules:
  0.0 30.0 jit_solution(10298353562494972593)
XLA Ops:
  0.0 0.0 copy-start
  0.0 0.7 %copy-done = s32[32,32]{1,0:T(8,128)S(1)} copy-done((s32[32,32]{1,0:T(8,128)S(1)}, s32[32,32]{1,0:T(8,128)}, u32[]{:S(2)}) %copy-start) | copy-done | bytes 4120
  0.7 28.7 %shard_map.46 = bf16[128,256]{1,0:T(8,128)(2,1)S(1)} custom-call(bf16[128,256]{1,0:T(8,128)(2,1)} %bitcast.5, bf16[128,256]{1,0:T(8,128)(2,1)} %bitcast.6, bf16[128,256]{1,0:T(8,128)(2,1)} %bitcast.7, s32[32,32]{1,0:T(8,128)S(1)} %copy-done), custom_call_target="tpu_custom_call" | custom-call | tf_op jit(solution)/shard_map/pallas_call | solution.py:295
  29.4 0.6 %copy.6 = bf16[1,128,256]{2,1,0:T(8,128)(2,1)} copy(bf16[1,128,256]{2,1,0:T(8,128)(2,1)S(1)} %bitcast.4) | data formatting | bytes 131072
Async XLA Ops:
  0.0 0.7 %copy-start = (s32[32,32]{1,0:T(8,128)S(1)}, s32[32,32]{1,0:T(8,128)}, u32[]{:S(2)}) copy-start(s32[32,32]{1,0:T(8,128)} %band_ref.1) | copy-start | bytes 12292

commit v3 on v2

--- a/solution.py
+++ b/solution.py
@@ -97,6 +97,7 @@
             remote(st_send.at[part, k - 1, h], st_recv.at[part, there, h], s_ss.at[part, there, h], s_rs.at[part, there, h], to),
         )
 
+    frame = z * YN + y
     loads[0].wait()
     vz[0] = v_in[...].T
     loads[1].wait()
@@ -106,30 +107,39 @@
         for h in range(HEADS):
             go(z_copy(1, h, kind, 0, 1))
             go(z_copy(7, h, kind, 0, -1))
+
+    pieces = [(h, kind) for h in range(HEADS) for kind in (K, V)]
+    before = [n_copy(1, h, kind, kz.at[0], vz.at[0], dy=1) for h, kind in pieces]
+    after = [n_copy(3, h, kind, kz.at[0], vz.at[0], dy=-1) for h, kind in pieces]
+
+    @pl.when((y < YN - 1))
+    def _():
+        for copy in before:
+            copy.start()
+
+    @pl.when(y > 0)
+    def _():
+        for copy in after:
+            copy.start()
+
+    for h, kind in pieces:
+        go(n_copy(0, h, kind, kz.at[0], vz.at[0], dc=1))
+
+    @pl.when(frame == 0)
+    def _():
+        kn[1:3] = jnp.zeros((2,) + kn.shape[1:], kn.dtype)
+        vn[1:3] = jnp.zeros((2,) + vn.shape[1:], vn.dtype)
+
+    @pl.when(frame == FRAMES - 1)
+    def _():
+        kn[3:5] = jnp.zeros((2,) + kn.shape[1:], kn.dtype)
+        vn[3:5] = jnp.zeros((2,) + vn.shape[1:], vn.dtype)
 
     loads[2].wait()
     q_own[...] = q_in[...].T
     for k in (2, 1, 3):
         go(q_copy(NEAR, k, XN))
         go(q_copy(FAR, k, YN))
-    pieces = [(h, kind) for h in range(HEADS) for kind in (K, V)]
-    before = [n_copy(1, h, kind, kz.at[0], vz.at[0], dy=1) for h, kind in pieces]
-    after = [n_copy(3, h, kind, kz.at[0], vz.at[0], dy=-1) for h, kind in pieces]
-    started.extend(before + after)
-
-    @pl.when(y < YN - 1)
-    def _():
-        for copy in before:
-            copy.start()
-
-    @pl.when(y > 0)
-    def _():
-        for copy in after:
-            copy.start()
-
-    for h, kind in pieces:
-        go(n_copy(0, h, kind, kz.at[0], vz.at[0], dc=1))
-
     loads[3].wait()
     lane = lax.broadcasted_iota(jnp.int32, (1, 4 * ROWS), 1) // ROWS
 
@@ -139,7 +149,6 @@
             row = jnp.where(lane == k, cells[k], row)
         return row
 
-    frame = z * YN + y
     for slot in range(ZN):
         key_frame = lax.rem(z + (ZN - slot), ZN) * YN + y
         cells = []
@@ -161,7 +170,7 @@
                 cells.append(jnp.where(seen, 0.0, HIDE).astype(jnp.float32))
             bias[ZN + step * CN + other] = row_of(cells)
 
-    def update(part, h, blocks, first):
+    def update(part, h, blocks, first, before_values=lambda: None):
         cols = pl.ds(h * HD, HD)
         qt = jnp.concatenate([q_own[cols]] + [q_set[part, k, cols] for k in range(3)], axis=1)
         rows = [bias[b] for _, _, b in blocks]
@@ -171,20 +180,23 @@
         new = jnp.maximum(old, high)
         weights = [jnp.exp2((s - (new - r)) * EXP2_SCALE) for s, r in zip(scores, rows)]
         add = functools.reduce(jnp.add, [jnp.sum(w, axis=0, keepdims=True) for w in weights])
-        wt = jnp.concatenate([w.astype(jnp.bfloat16) for w in weights], axis=0)
-        vt = jnp.concatenate([values[cols] for _, values, _ in blocks], axis=1)
-        out = jnp.dot(vt, wt, preferred_element_type=jnp.float32)
         top[part, h] = new
         if first:
             total[part, h] = add
-            acc[part, h] = out
         else:
             factor = jnp.exp2((old - new) * EXP2_SCALE)
             total[part, h] = total[part, h] * factor + add
+        wt = jnp.concatenate([w.astype(jnp.bfloat16) for w in weights], axis=0)
+        before_values()
+        vt = jnp.concatenate([values[cols] for _, values, _ in blocks], axis=1)
+        out = jnp.dot(vt, wt, preferred_element_type=jnp.float32)
+        if first:
+            acc[part, h] = out
+        else:
             acc[part, h] = acc[part, h] * factor + out
 
-    def far(h, slots, first=False):
-        update(FAR, h, [(kz.at[s], vz.at[s], s) for s in slots], first)
+    def far(h, slots, first=False, before_values=lambda: None):
+        update(FAR, h, [(kz.at[s], vz.at[s], s) for s in slots], first, before_values)
 
     def near(h, refs, first=False):
         update(NEAR, h, [(keys, values, b) for keys, values, b in refs], first)
@@ -204,16 +216,31 @@
             z_wait(1, h, kind)
             go(z_copy(2, h, kind, 1, 1))
 
-            @pl.when(y == YN - 1)
+            @pl.when((y == YN - 1) & (z > 0))
             def _(h=h, kind=kind):
                 n_copy(1, h, kind, kz.at[1], vz.at[1], dy=1).start()
 
             z_wait(7, h, kind)
             go(z_copy(6, h, kind, 7, -1))
 
-            @pl.when(y == 0)
+            @pl.when((y == 0) & (z < ZN - 1))
             def _(h=h, kind=kind):
                 n_copy(3, h, kind, kz.at[7], vz.at[7], dy=-1).start()
+
+    def hand_over(slot, h):
+        for kind in (K, V):
+            n_wait(slot, h, kind)
+            n_copy(slot + 1, h, kind, kn.at[slot], vn.at[slot], dc=1).start()
+
+    @pl.when(y > 0)
+    def _():
+        for h in range(HEADS):
+            hand_over(1, h)
+
+    @pl.when(y < YN - 1)
+    def _():
+        for h in range(HEADS):
+            hand_over(3, h)
 
     for h, kind in pieces:
         n_wait(0, h, kind)
@@ -221,9 +248,6 @@
         q_copy(NEAR, k, XN).wait_recv()
     for h in range(HEADS):
         near(h, [(kz.at[0], vz.at[0], ZN + 2), (kn.at[0], vn.at[0], ZN + 3)], first=True)
-    for k in range(1, YN):
-        q_copy(FAR, k, YN).wait_recv()
-    far(0, (0, 1, 7), first=True)
 
     for h in range(HEADS):
         for kind in (K, V):
@@ -236,25 +260,38 @@
             if kind == V:
                 go(z_copy(4, h, kind, 6, -2))
 
-    for h, kind in pieces:
-        for slot in (1, 3):
-            n_wait(slot, h, kind)
-            go(n_copy(slot + 1, h, kind, kn.at[slot], vn.at[slot], dc=1))
-    far(1, (0, 1, 7), first=True)
-    for h in range(HEADS):
-        far(h, (2, 6))
+        @pl.when((y == 0) & (z > 0))
+        def _(h=h):
+            hand_over(1, h)
+
+        @pl.when((y == YN - 1) & (z < ZN - 1))
+        def _(h=h):
+            hand_over(3, h)
+
+
+    for k in range(1, YN):
+        q_copy(FAR, k, YN).wait_recv()
+    for h in range(HEADS):
+        far(h, (0, 1, 7, 2, 6), first=True)
     for h in range(HEADS):
         for slot in (2, 4):
             for kind in (K, V):
-                n_wait(slot, h, kind)
-        near(h, [(kn.at[1], vn.at[1], ZN), (kn.at[2], vn.at[2], ZN + 1)])
-        near(h, [(kn.at[3], vn.at[3], ZN + 4), (kn.at[4], vn.at[4], ZN + 5)])
+                @pl.when(frame != (0 if slot == 2 else FRAMES - 1))
+                def _(h=h, kind=kind, slot=slot):
+                    n_wait(slot, h, kind)
+                    n_copy(slot, h, kind, kn.at[slot - 1], vn.at[slot - 1], dc=1).wait_send()
+
+        near(h, [(kn.at[1], vn.at[1], ZN), (kn.at[2], vn.at[2], ZN + 1), (kn.at[3], vn.at[3], ZN + 4), (kn.at[4], vn.at[4], ZN + 5)])
         send_out(NEAR, h, XN)
     for h in range(HEADS):
         for slot in (3, 5, 4):
-            for kind in (K, V):
-                z_wait(slot, h, kind)
-        far(h, (4, 3, 5))
+            z_wait(slot, h, K)
+
+        def values_wait(h=h):
+            for slot in (3, 5, 4):
+                z_wait(slot, h, V)
+
+        far(h, (3, 5, 4), before_values=values_wait)
         send_out(FAR, h, YN)
 
     def merged(h, state, part):
@@ -285,6 +322,16 @@
         o_ref[:, h * HD:(h + 1) * HD] = (out / count).T.astype(jnp.bfloat16)
     for copy in started:
         copy.wait_send()
+
+    @pl.when((y < YN - 1) | (z > 0))
+    def _():
+        for copy in before:
+            copy.wait_send()
+
+    @pl.when((y > 0) | (z < ZN - 1))
+    def _():
+        for copy in after:
+            copy.wait_send()
 
 
 def shards(queries, keys, values, band):

time: 30.2 us -> 29 us (0.960)
  the two profiles are of different devices: /device:TPU:1 before, /device:TPU:6 now
where the time goes in v3:
time: 29 us; the launch traced here: 28.7 us
  Pallas kernels  27.4 us (94%)
  local copies, waits for them, and re-layouts  1.35 us (5%)
    pallas_call x1, Pallas kernels, shards(): pl.pallas_call(kernel, out_shape=jax.ShapeDtypeStruct((ROWS, width), bf16...  27.4 us
    unnamed x3, local copies, waits for them, and re-layouts  1.35 us

profile of v3, /device:TPU:6, one launch (start us, length us, event | category | flops | bytes accessed | tf_op | source)
XLA Modules:
  0.0 28.7 jit_solution(1671617987166124033)
XLA Ops:
  0.0 0.0 copy-start
  0.0 0.7 %copy-done = s32[32,32]{1,0:T(8,128)S(1)} copy-done((s32[32,32]{1,0:T(8,128)S(1)}, s32[32,32]{1,0:T(8,128)}, u32[]{:S(2)}) %copy-start) | copy-done | bytes 4120
  0.7 27.4 %shard_map.46 = bf16[128,256]{1,0:T(8,128)(2,1)S(1)} custom-call(bf16[128,256]{1,0:T(8,128)(2,1)} %bitcast.5, bf16[128,256]{1,0:T(8,128)(2,1)} %bitcast.6, bf16[128,256]{1,0:T(8,128)(2,1)} %bitcast.7, s32[32,32]{1,0:T(8,128)S(1)} %copy-done), custom_call_target="tpu_custom_call" | custom-call | tf_op jit(solution)/shard_map/pallas_call | solution.py:342
  28.1 0.6 %copy.6 = bf16[1,128,256]{2,1,0:T(8,128)(2,1)} copy(bf16[1,128,256]{2,1,0:T(8,128)(2,1)S(1)} %bitcast.4) | data formatting | bytes 131072
Async XLA Ops:
  0.0 0.7 %copy-start = (s32[32,32]{1,0:T(8,128)S(1)}, s32[32,32]{1,0:T(8,128)}, u32[]{:S(2)}) copy-start(s32[32,32]{1,0:T(8,128)} %band_ref.1) | copy-start | bytes 12292

commit v4 on v3

--- a/solution.py
+++ b/solution.py
@@ -317,21 +317,22 @@
         f1 = jnp.exp2((one[0] - new) * EXP2_SCALE)
         f2 = jnp.exp2((two[0] - new) * EXP2_SCALE)
         states.append(merged(h, (new, one[1] * f1 + two[1] * f2, one[2] * f1 + two[2] * f2), NEAR))
+    for copy in started:
+        copy.wait_send()
+
+    @pl.when((y < YN - 1) | (z > 0))
+    def _():
+        for copy in before:
+            copy.wait_send()
+
+    @pl.when((y > 0) | (z < ZN - 1))
+    def _():
+        for copy in after:
+            copy.wait_send()
+
     for h in range(HEADS):
         _, count, out = merged(h, states[h], FAR)
         o_ref[:, h * HD:(h + 1) * HD] = (out / count).T.astype(jnp.bfloat16)
-    for copy in started:
-        copy.wait_send()
-
-    @pl.when((y < YN - 1) | (z > 0))
-    def _():
-        for copy in before:
-            copy.wait_send()
-
-    @pl.when((y > 0) | (z < ZN - 1))
-    def _():
-        for copy in after:
-            copy.wait_send()
 
 
 def shards(queries, keys, values, band):

time: 29 us -> 28.8 us (level)
  no operation moved by 1% of the time
where the time goes in v4:
time: 28.8 us; the launch traced here: 28.6 us
  Pallas kernels  27.3 us (95%)
  local copies, waits for them, and re-layouts  1.35 us (5%)
    pallas_call x1, Pallas kernels, shards(): pl.pallas_call(kernel, out_shape=jax.ShapeDtypeStruct((ROWS, width), bf16...  27.3 us
    unnamed x3, local copies, waits for them, and re-layouts  1.35 us

profile of v4, /device:TPU:6, one launch (start us, length us, event | category | flops | bytes accessed | tf_op | source)
XLA Modules:
  0.0 28.6 jit_solution(18038333112972428296)
XLA Ops:
  0.0 0.0 copy-start
  0.0 0.7 %copy-done = s32[32,32]{1,0:T(8,128)S(1)} copy-done((s32[32,32]{1,0:T(8,128)S(1)}, s32[32,32]{1,0:T(8,128)}, u32[]{:S(2)}) %copy-start) | copy-done | bytes 4120
  0.7 27.3 %shard_map.46 = bf16[128,256]{1,0:T(8,128)(2,1)S(1)} custom-call(bf16[128,256]{1,0:T(8,128)(2,1)} %bitcast.5, bf16[128,256]{1,0:T(8,128)(2,1)} %bitcast.6, bf16[128,256]{1,0:T(8,128)(2,1)} %bitcast.7, s32[32,32]{1,0:T(8,128)S(1)} %copy-done), custom_call_target="tpu_custom_call" | custom-call | tf_op jit(solution)/shard_map/pallas_call | solution.py:343
  28.0 0.6 %copy.6 = bf16[1,128,256]{2,1,0:T(8,128)(2,1)} copy(bf16[1,128,256]{2,1,0:T(8,128)(2,1)S(1)} %bitcast.4) | data formatting | bytes 131072
Async XLA Ops:
  0.0 0.7 %copy-start = (s32[32,32]{1,0:T(8,128)S(1)}, s32[32,32]{1,0:T(8,128)}, u32[]{:S(2)}) copy-start(s32[32,32]{1,0:T(8,128)} %band_ref.1) | copy-start | bytes 12292

commit v5 on v4

--- a/solution.py
+++ b/solution.py
@@ -112,15 +112,14 @@
     before = [n_copy(1, h, kind, kz.at[0], vz.at[0], dy=1) for h, kind in pieces]
     after = [n_copy(3, h, kind, kz.at[0], vz.at[0], dy=-1) for h, kind in pieces]
 
-    @pl.when((y < YN - 1))
-    def _():
-        for copy in before:
-            copy.start()
-
-    @pl.when(y > 0)
-    def _():
-        for copy in after:
-            copy.start()
+    for one, other in zip(before, after):
+        @pl.when(y < YN - 1)
+        def _(one=one):
+            one.start()
+
+        @pl.when(y > 0)
+        def _(other=other):
+            other.start()
 
     for h, kind in pieces:
         go(n_copy(0, h, kind, kz.at[0], vz.at[0], dc=1))
@@ -227,8 +226,8 @@
             def _(h=h, kind=kind):
                 n_copy(3, h, kind, kz.at[7], vz.at[7], dy=-1).start()
 
-    def hand_over(slot, h):
-        for kind in (K, V):
+    def hand_over(slot, h, kinds=(K, V)):
+        for kind in kinds:
             n_wait(slot, h, kind)
             n_copy(slot + 1, h, kind, kn.at[slot], vn.at[slot], dc=1).start()
 
@@ -252,21 +251,21 @@
     for h in range(HEADS):
         for kind in (K, V):
             z_wait(2, h, kind)
-            go(z_copy(3, h, kind, 2, 1))
             if kind == K:
                 go(z_copy(4, h, kind, 2, 2))
+            go(z_copy(3, h, kind, 2, 1))
             z_wait(6, h, kind)
-            go(z_copy(5, h, kind, 6, -1))
             if kind == V:
                 go(z_copy(4, h, kind, 6, -2))
-
-        @pl.when((y == 0) & (z > 0))
-        def _(h=h):
-            hand_over(1, h)
-
-        @pl.when((y == YN - 1) & (z < ZN - 1))
-        def _(h=h):
-            hand_over(3, h)
+            go(z_copy(5, h, kind, 6, -1))
+
+            @pl.when((y == 0) & (z > 0))
+            def _(h=h, kind=kind):
+                hand_over(1, h, (kind,))
+
+            @pl.when((y == YN - 1) & (z < ZN - 1))
+            def _(h=h, kind=kind):
+                hand_over(3, h, (kind,))
 
 
     for k in range(1, YN):

time: 28.8 us -> 28.8 us (level)
  no operation moved by 1% of the time
where the time goes in v5:
time: 28.8 us; the launch traced here: 28.7 us
  Pallas kernels  27.3 us (95%)
  local copies, waits for them, and re-layouts  1.35 us (5%)
    pallas_call x1, Pallas kernels, shards(): pl.pallas_call(kernel, out_shape=jax.ShapeDtypeStruct((ROWS, width), bf16...  27.3 us
    unnamed x3, local copies, waits for them, and re-layouts  1.35 us

profile of v5, /device:TPU:6, one launch (start us, length us, event | category | flops | bytes accessed | tf_op | source)
XLA Modules:
  0.0 28.7 jit_solution(12568227303380911340)
XLA Ops:
  0.0 0.0 copy-start
  0.0 0.7 %copy-done = s32[32,32]{1,0:T(8,128)S(1)} copy-done((s32[32,32]{1,0:T(8,128)S(1)}, s32[32,32]{1,0:T(8,128)}, u32[]{:S(2)}) %copy-start) | copy-done | bytes 4120
  0.7 27.3 %shard_map.46 = bf16[128,256]{1,0:T(8,128)(2,1)S(1)} custom-call(bf16[128,256]{1,0:T(8,128)(2,1)} %bitcast.5, bf16[128,256]{1,0:T(8,128)(2,1)} %bitcast.6, bf16[128,256]{1,0:T(8,128)(2,1)} %bitcast.7, s32[32,32]{1,0:T(8,128)S(1)} %copy-done), custom_call_target="tpu_custom_call" | custom-call | tf_op jit(solution)/shard_map/pallas_call | solution.py:342
  28.0 0.6 %copy.6 = bf16[1,128,256]{2,1,0:T(8,128)(2,1)} copy(bf16[1,128,256]{2,1,0:T(8,128)(2,1)S(1)} %bitcast.4) | data formatting | bytes 131072
Async XLA Ops:
  0.0 0.7 %copy-start = (s32[32,32]{1,0:T(8,128)S(1)}, s32[32,32]{1,0:T(8,128)}, u32[]{:S(2)}) copy-start(s32[32,32]{1,0:T(8,128)} %band_ref.1) | copy-start | bytes 12292
